TPU v7x, 32 devices: a whole 2x2x4 slice. The times are simulated.
32 devices in a mesh: groups: 2 (over x), expert: 16 (over z, y, core).
Axes of the slice: x: 2, y: 2, z: 4, core: 2. Of those that a mesh axis runs over, the one named last changes fastest.
Arguments:
- tokens: bfloat16 [4096, 1536], P(('groups', 'expert')), parts along dimension 0, may hold values from -6 to 6
- target: bfloat16 [4096, 1536], P(('groups', 'expert')), parts along dimension 0, may hold values from -6 to 6
- expert_ids: int32 [4096, 8], P(('groups', 'expert')), parts along dimension 0, may hold values from 0 to 31, all different within a row; in each aligned block of 128 rows (0 to 127, 128 to 255, ...) at most 48 rows name the same one
- gate_weights: float32 [4096, 8], P(('groups', 'expert')), parts along dimension 0, may hold values from 0.05 to 0.5
- w_gate: bfloat16 [32, 1536, 384], P('expert'), may hold values from -0.15625 to 0.15625
- w_up: bfloat16 [32, 1536, 384], P('expert'), may hold values from -0.15625 to 0.15625
- w_down: bfloat16 [32, 384, 1536], P('expert'), may hold values from -0.3125 to 0.3125
- dir_gate: bfloat16 [32, 1536, 384], P('expert'), may hold values from -0.15625 to 0.15625
- dir_up: bfloat16 [32, 1536, 384], P('expert'), may hold values from -0.15625 to 0.15625
- dir_down: bfloat16 [32, 384, 1536], P('expert'), may hold values from -0.3125 to 0.3125
Outputs:
- hv_gate: bfloat16 [64, 1536, 384], P(('groups', 'expert')), parts along dimension 0
- hv_up: bfloat16 [64, 1536, 384], P(('groups', 'expert')), parts along dimension 0
- hv_down: bfloat16 [64, 384, 1536], P(('groups', 'expert')), parts along dimension 0
There are 2 independent parts, one for each index of `groups`. A program takes and returns all parts, laid end to end along the dimension named above; an argument that names none is the same for every part. Nothing has to cross between parts.
Inputs may be any that keep to these rules, and one draw needn't show every extreme that they name: `expert_ids`: each token names 8 different experts. In the rows of one index of expert no expert is named more than 48 times, and in some such rows one expert is named exactly 48 times.
All inputs are finite; a program needn't handle non-finite values.
Results may differ from a plain program's by a relative error of at most 0.0068.
Values may be sent and summed in bfloat16 or wider, within the bound.
No kernel may reach another device: no remote copies, remote signals or barrier semaphores. Data moves between devices by JAX's collectives and lax.ppermute only.
A program may use at most 128 MiB of HBM per device.

v0:
```python
import jax
import jax.numpy as jnp
from jax import lax
from jax.sharding import PartitionSpec as P


def silu_parts(preact):
    sigmoid_value = jax.nn.sigmoid(preact)
    activation = preact * sigmoid_value
    first_deriv = sigmoid_value * (1.0 + preact * (1.0 - sigmoid_value))
    second_deriv = (
        sigmoid_value * (1.0 - sigmoid_value) * (2.0 + preact * (1.0 - 2.0 * sigmoid_value))
    )
    return (activation, first_deriv, second_deriv)


def project(left, right, form):
    return jnp.einsum(form, left, right, preferred_element_type=jnp.float32)


def local(
    tokens, target, expert_ids, gate_weights, w_gate, w_up, w_down, dir_gate, dir_up, dir_down
):
    devices = lax.axis_size("expert")
    exp_dev = w_gate.shape[0]
    experts = exp_dev * devices
    tok_rows, top_k = expert_ids.shape
    model_width = tokens.shape[1]
    capacity = max(2, 3 * tok_rows * top_k // (2 * experts))
    slot_count = exp_dev * devices * capacity
    route_ids = expert_ids.reshape(-1)
    expert_names = jnp.arange(experts, dtype=jnp.int32)
    hit_table = (route_ids[:, None] == expert_names[None, :]).astype(jnp.int32)
    position = jnp.sum(jnp.cumsum(hit_table, 0) * hit_table, 1) - 1
    target_slot = (route_ids % exp_dev * devices + route_ids // exp_dev) * capacity + position

    def to_slots(entries):
        placed = jnp.zeros((slot_count, model_width), jnp.bfloat16).at[target_slot].set(entries)
        return placed.reshape(exp_dev, devices, capacity, model_width)

    def from_slots(buffer):
        picked = buffer.reshape(slot_count, model_width)[target_slot]
        return picked.reshape(tok_rows, top_k, model_width).astype(jnp.float32)

    def flat_rows(tensor):
        return tensor.reshape(exp_dev, devices * capacity, model_width)

    def by_source(tensor):
        return tensor.reshape(exp_dev, devices, capacity, model_width)

    dispatched = to_slots(jnp.repeat(tokens, top_k, axis=0))
    expert_rows = flat_rows(
        lax.all_to_all(dispatched, "expert", split_axis=1, concat_axis=1, tiled=True)
    )
    pre_gate = project(expert_rows, w_gate, "erd,edf->erf")
    pre_up = project(expert_rows, w_up, "erd,edf->erf")
    dot_gate = project(expert_rows, dir_gate, "erd,edf->erf")
    dot_up = project(expert_rows, dir_up, "erd,edf->erf")
    activation, first_deriv, second_deriv = silu_parts(pre_gate)
    hidden = (activation * pre_up).astype(jnp.bfloat16)
    out = project(hidden, w_down, "erf,efd->erd").astype(jnp.bfloat16)
    hidden_dot = (first_deriv * dot_gate * pre_up + activation * dot_up).astype(jnp.bfloat16)
    out_dot = (
        project(hidden_dot, w_down, "erf,efd->erd") + project(hidden, dir_down, "erf,efd->erd")
    ).astype(jnp.bfloat16)
    hidden_dot, out_dot = (hidden_dot, out_dot)
    returned, returned_dot = (
        lax.all_to_all(by_source(out), "expert", split_axis=1, concat_axis=1, tiled=True),
        lax.all_to_all(by_source(out_dot), "expert", split_axis=1, concat_axis=1, tiled=True),
    )
    merged = jnp.sum(gate_weights[:, :, None] * from_slots(returned), 1)
    merged_dot = jnp.sum(gate_weights[:, :, None] * from_slots(returned_dot), 1)
    residual = merged - target.astype(jnp.float32)
    cot_send = to_slots(
        (gate_weights[:, :, None] * residual[:, None, :])
        .astype(jnp.bfloat16)
        .reshape(-1, model_width)
    )
    cot_dot_send = to_slots(
        (gate_weights[:, :, None] * merged_dot[:, None, :])
        .astype(jnp.bfloat16)
        .reshape(-1, model_width)
    )
    cotangent, cotangent_dot = (
        lax.all_to_all(cot_send, "expert", split_axis=1, concat_axis=1, tiled=True),
        lax.all_to_all(cot_dot_send, "expert", split_axis=1, concat_axis=1, tiled=True),
    )
    cotangent = flat_rows(cotangent)
    cotangent_dot = flat_rows(cotangent_dot)
    grad_hidden = project(cotangent, w_down, "erd,efd->erf")
    down_first = project(hidden_dot, cotangent, "erf,erd->efd")
    grad_dot = project(cotangent_dot, w_down, "erd,efd->erf") + project(
        cotangent, dir_down, "erd,efd->erf"
    )
    gate_dot = (
        grad_dot * first_deriv * pre_up
        + grad_hidden * second_deriv * dot_gate * pre_up
        + grad_hidden * first_deriv * dot_up
    ).astype(jnp.bfloat16)
    up_dot = (grad_dot * activation + grad_hidden * first_deriv * dot_gate).astype(jnp.bfloat16)
    hv_gate = project(expert_rows, gate_dot, "erd,erf->edf").astype(jnp.bfloat16)
    hv_up = project(expert_rows, up_dot, "erd,erf->edf").astype(jnp.bfloat16)
    hv_down = (down_first + project(hidden, cotangent_dot, "erf,erd->efd")).astype(jnp.bfloat16)
    return (hv_gate, hv_up, hv_down)


def solution(mesh):
    in_specs = (
        P(("groups", "expert"), None),
        P(("groups", "expert"), None),
        P(("groups", "expert"), None),
        P(("groups", "expert"), None),
        P("expert", None, None),
        P("expert", None, None),
        P("expert", None, None),
        P("expert", None, None),
        P("expert", None, None),
        P("expert", None, None),
    )
    out_specs = (
        P(("groups", "expert"), None, None),
        P(("groups", "expert"), None, None),
        P(("groups", "expert"), None, None),
    )
    return jax.shard_map(local, mesh=mesh, in_specs=in_specs, out_specs=out_specs, check_vma=False)
```

profile of v0, /device:TPU:13, one launch (start us, length us, event | category | flops | bytes accessed | tf_op | source)
XLA Modules:
  0.0 614.4 jit_solution(15384847664376012049)
XLA Ops:
  0.6 0.9 copy.47
  1.8 0.1 reshape.200
  1.9 9.0 %reduce-window.6 = s32[32,8,128]{2,1,0:T(8,128)S(1)} reduce-window(s32[32,8,128]{2,1,0:T(8,128)S(1)} %fusion.35, s32[]{:T(128)} %constant.38.clone.1), window={size=1x1x128 pad=0_0x0_0x127_0}, to_apply=%region_0.0 | reduce-window | flops 4161536 | bytes 262148 | tf_op jit(solution)/shard_map/reduce-window
  11.0 0.1 copy.50
  11.2 0.1 broadcast_add_fusion
  11.5 8.6 %scatter_custom_fusion = bf16[1536,1536]{1,0:T(8,128)(2,1)} fusion(s32[1024]{0:T(1024)S(1)} %bitcast.98, bf16[]{:T(256)} %constant.37.clone.1, bf16[128,1536]{1,0:T(8,128)(2,1)} %param.10), kind=kCustom, calls=%fused_computation.23 | custom fusion | bytes 5111810 | tf_op jit(solution)/shard_map/scatter | solution.py:38
  20.1 2.6 copy.52
  22.7 110.4 %all_to_all.25 = bf16[2,16,48,1536]{3,2,0,1:T(8,128)(2,1)S(1)} all-to-all(bf16[2,16,48,1536]{3,2,0,1:T(8,128)(2,1)S(1)} %copy.52), channel_id=1, replica_groups=mesh['groups'=2,'expert'=16] {'expert'}, dimensions={1} | all-to-all | bytes 9437184 | tf_op jit(solution)/shard_map/all_to_all | solution.py:53
  133.1 0.4 copy.53
  133.5 2.1 copy-done.10
  135.6 2.6 fusion.43
  138.2 2.6 fusion.44
  140.8 2.6 fusion.45
  143.5 5.1 add_convert_fusion.3
  148.6 2.8 convolution_convert_fusion
  151.4 2.4 copy.60
  153.9 5.3 all-to-all-start.3
  159.2 4.0 fusion.46
  163.2 2.8 add_convert_fusion
  166.1 2.7 copy.56
  168.7 94.2 %all-to-all-done.3 = bf16[2,16,48,1536]{3,2,0,1:T(8,128)(2,1)} async-done(((bf16[2,16,48,1536]{3,2,0,1:T(8,128)(2,1)}), bf16[2,16,48,1536]{3,2,0,1:T(8,128)(2,1)}, u32[]{:S(2)}, u32[]{:S(2)}) %all-to-all-start.3) | async-done | bytes 4718624 | tf_op jit(solution)/shard_map/all_to_all | solution.py:68
  262.9 5.2 all-to-all-start.1
  268.1 0.1 copy.54
  268.3 4.9 copy.61
  273.3 10.2 %gather_fusion.1 = bf16[1024,1536]{1,0:T(8,128)(2,1)} fusion(bf16[1536,1536]{1,0:T(8,128)(2,1)} %bitcast.75, s32[1024]{0:T(1024)S(1)} %broadcast_clamp_fusion), kind=kCustom, calls=%fused_computation.1 | custom fusion | bytes 6295552 | tf_op jit(solution)/shard_map/gather | solution.py:42
  283.5 4.8 fusion.1
  288.3 8.8 %scatter_custom_fusion.2 = bf16[1536,1536]{1,0:T(8,128)(2,1)} fusion(s32[1024]{0:T(1024)S(1)} %bitcast.100, f32[128,1536]{1,0:T(8,128)S(1)} %convert_subtract_fusion, f32[1024]{0:T(1024)S(1)} %mul.141, bf16[]{:T(256)} %constant.37.clone.1), kind=kCustom, calls=%fused_computation.21 | custom fusion | flops 3145728 | bytes 5509122 | tf_op jit(solution)/shard_map/scatter | solution.py:38
  297.2 4.9 copy.62
  302.1 69.6 %all-to-all-done.1 = bf16[2,16,48,1536]{3,2,0,1:T(8,128)(2,1)} async-done(((bf16[2,16,48,1536]{3,2,0,1:T(8,128)(2,1)}), bf16[2,16,48,1536]{3,2,0,1:T(8,128)(2,1)}, u32[]{:S(2)}, u32[]{:S(2)}) %all-to-all-start.1) | async-done | bytes 4718624 | tf_op jit(solution)/shard_map/all_to_all | solution.py:69
  371.7 5.2 all-to-all-start.4
  376.9 4.9 copy.57
  381.8 10.2 %gather_fusion = bf16[1024,1536]{1,0:T(8,128)(2,1)} fusion(bf16[1536,1536]{1,0:T(8,128)(2,1)} %bitcast.74, s32[1024]{0:T(1024)S(1)} %broadcast_clamp_fusion), kind=kCustom, calls=%fused_computation | custom fusion | bytes 6295552 | tf_op jit(solution)/shard_map/gather | solution.py:42
  392.1 5.6 fusion.4
  397.7 9.3 %scatter_custom_fusion.1 = bf16[1536,1536]{1,0:T(8,128)(2,1)} fusion(s32[1024]{0:T(1024)S(1)} %bitcast.101, bf16[1024,1536]{1,0:T(8,128)(2,1)} %fusion.4, bf16[]{:T(256)} %constant.37.clone.1), kind=kCustom, calls=%fused_computation.42 | custom fusion | bytes 4719104 | tf_op jit(solution)/shard_map/scatter | solution.py:38
  406.9 4.9 copy.58
  411.8 68.7 %all-to-all-done.4 = bf16[2,16,48,1536]{3,2,0,1:T(8,128)(2,1)} async-done(((bf16[2,16,48,1536]{3,2,0,1:T(8,128)(2,1)}), bf16[2,16,48,1536]{3,2,0,1:T(8,128)(2,1)}, u32[]{:S(2)}, u32[]{:S(2)}) %all-to-all-start.4) | async-done | bytes 4718624 | tf_op jit(solution)/shard_map/all_to_all | solution.py:85
  480.5 5.3 all-to-all-start.2
  485.8 2.7 copy.63
  488.6 4.3 fusion.49
  492.9 4.1 fusion.48
  497.0 92.4 %all-to-all-done.2 = bf16[2,16,48,1536]{3,2,0,1:T(8,128)(2,1)} async-done(((bf16[2,16,48,1536]{3,2,0,1:T(8,128)(2,1)}), bf16[2,16,48,1536]{3,2,0,1:T(8,128)(2,1)}, u32[]{:S(2)}, u32[]{:S(2)}) %all-to-all-start.2) | async-done | bytes 4718624 | tf_op jit(solution)/shard_map/all_to_all | solution.py:86
  589.3 2.6 copy.59
  592.0 2.6 fusion.47
  594.7 3.5 add_convert_fusion.1
  598.3 2.7 convolution_add_fusion
  601.0 0.5 copy-done.21
  601.5 4.5 convolution_convert_fusion.1
  606.0 7.9 %convolution_convert_fusion.2 = bf16[2,1536,384]{2,1,0:T(8,128)(2,1)} fusion(bf16[2,768,1536]{2,1,0:T(8,128)(2,1)S(1)} %bitcast.87, f32[2,768,384]{2,1,0:T(8,128)} %copy-done.20, f32[2,768,384]{2,1,0:T(8,128)S(1)} %copy-done.19, f32[2,768,384]{2,1,0:T(8,128)} %fusion.48, f32[2,768,384]{2,1,0:T(8,128)} %get-tuple-element.5, ...), kind=kOutput, calls=%fused_computation.20 | convolution fusion | flops 1826095104 | bytes 21233664 | tf_op jit(solution)/shard_map/erd,erf->edf/dot_general | solution.py:18
  (65 shorter events, 0.8 us)
Async XLA Ops:
  0.6 148.0 %copy-start = (bf16[2,384,1536]{2,1,0:T(8,128)(2,1)S(1)}, bf16[2,384,1536]{2,1,0:T(8,128)(2,1)}, u32[]{:S(2)}) copy-start(bf16[2,384,1536]{2,1,0:T(8,128)(2,1)} %param.16) | copy-start | bytes 7077892
  133.1 2.5 copy-start.10
  133.5 10.0 %copy-start.1 = (bf16[2,16,48,1536]{3,2,1,0:T(8,128)(2,1)}, bf16[2,16,48,1536]{3,2,1,0:T(8,128)(2,1)S(1)}, u32[]{:S(2)}) copy-start(bf16[2,16,48,1536]{3,2,1,0:T(8,128)(2,1)S(1)} %copy.53) | copy-start | bytes 14155780
  135.6 2.6 copy-start.11
  138.2 5.3 copy-start.15
  138.2 2.6 copy-start.12
  140.8 2.7 copy-start.17
  140.8 2.7 copy-start.13
  143.5 5.1 copy-start.20
  148.6 14.6 %copy-start.5 = (bf16[2,768,384]{2,1,0:T(8,128)(2,1)}, bf16[2,768,384]{2,1,0:T(8,128)(2,1)S(1)}, u32[]{:S(2)}) copy-start(bf16[2,768,384]{2,1,0:T(8,128)(2,1)S(1)} %get-tuple-element.4) | copy-start | bytes 3538948
  153.9 109.0 %all-to-all-start.3 = ((bf16[2,16,48,1536]{3,2,0,1:T(8,128)(2,1)}), bf16[2,16,48,1536]{3,2,0,1:T(8,128)(2,1)}, u32[]{:S(2)}, u32[]{:S(2)}) async-start(bf16[2,16,48,1536]{3,2,0,1:T(8,128)(2,1)} %copy.60), calls=%async_computation.3 | async-start | bytes 9437184 | tf_op jit(solution)/shard_map/all_to_all | solution.py:68
  159.2 4.0 copy-start.3
  168.7 99.4 %copy-start.9 = (f32[128,8]{0,1:T(8,128)S(1)}, f32[128,8]{0,1:T(8,128)}, u32[]{:S(2)}) copy-start(f32[128,8]{0,1:T(8,128)} %param.13) | copy-start | bytes 12292
  262.9 108.8 %all-to-all-start.1 = ((bf16[2,16,48,1536]{3,2,0,1:T(8,128)(2,1)}), bf16[2,16,48,1536]{3,2,0,1:T(8,128)(2,1)}, u32[]{:S(2)}, u32[]{:S(2)}) async-start(bf16[2,16,48,1536]{3,2,0,1:T(8,128)(2,1)} %copy.56), calls=%async_computation.1 | async-start | bytes 9437184 | tf_op jit(solution)/shard_map/all_to_all | solution.py:69
  283.5 4.8 copy-start.8
  371.7 108.8 %all-to-all-start.4 = ((bf16[2,16,48,1536]{3,2,0,1:T(8,128)(2,1)}), bf16[2,16,48,1536]{3,2,0,1:T(8,128)(2,1)}, u32[]{:S(2)}, u32[]{:S(2)}) async-start(bf16[2,16,48,1536]{3,2,0,1:T(8,128)(2,1)} %copy.62), calls=%async_computation.4 | async-start | bytes 9437184 | tf_op jit(solution)/shard_map/all_to_all | solution.py:85
  480.5 108.8 %all-to-all-start.2 = ((bf16[2,16,48,1536]{3,2,0,1:T(8,128)(2,1)}), bf16[2,16,48,1536]{3,2,0,1:T(8,128)(2,1)}, u32[]{:S(2)}, u32[]{:S(2)}) async-start(bf16[2,16,48,1536]{3,2,0,1:T(8,128)(2,1)} %copy.58), calls=%async_computation.2 | async-start | bytes 9437184 | tf_op jit(solution)/shard_map/all_to_all | solution.py:86
  485.8 2.8 copy-start.7
  488.5 4.3 copy-start.2
  592.0 2.6 copy-start.6
  592.0 2.7 copy-start.14
  592.0 6.2 %slice-start.2 = ((s8[4718592]{0:T(1024)(128)(4,1)}), s8[4194304]{0:T(1024)(128)(4,1)S(1)}, s32[]{:S(2)}) async-start(s8[4718592]{0:T(1024)(128)(4,1)} %bitcast.90), calls=%async_computation.7 | async-start | bytes 8388608
  594.7 3.5 slice-start.3
  594.7 3.5 copy-start.4
  594.7 6.3 %slice-start = ((s8[4718592]{0:T(1024)(128)(4,1)}), s8[4194304]{0:T(1024)(128)(4,1)S(1)}, s32[]{:S(2)}) async-start(s8[4718592]{0:T(1024)(128)(4,1)} %bitcast.84), calls=%async_computation.5 | async-start | bytes 8388608
  598.2 2.7 slice-start.1
  598.3 2.7 copy-start.16
  598.3 2.7 copy-start.18
  598.3 3.2 copy-start.21
  601.5 4.5 copy-start.19
where the time goes:
time: 620 us; the launch traced here: 614 us
  waiting for transfers between devices  325 us (52%)
  blocking collectives  110 us (18%)
  local copies, waits for them, and re-layouts  75.9 us (12%)
  matrix products  52.2 us (8%)
  other arithmetic  28.5 us (5%)
  starting transfers between devices  21.1 us (3%)
    all_to_all x1, blocking collectives, local(): lax.all_to_all(dispatched, 'expert', split_axis=1, concat_axis=1, tiled=T...  110 us
    all_to_all x1, waiting for transfers between devices, local(): lax.all_to_all(by_source(out), 'expert', split_axis=1, concat_axis=1, til...  94.2 us
    all_to_all x1, waiting for transfers between devices, local(): lax.all_to_all(cot_dot_send, 'expert', split_axis=1, concat_axis=1, tiled...  92.4 us
    all_to_all x1, waiting for transfers between devices, local(): lax.all_to_all(by_source(out_dot), 'expert', split_axis=1, concat_axis=1,...  69.6 us
    all_to_all x1, waiting for transfers between devices, local(): lax.all_to_all(cot_send, 'expert', split_axis=1, concat_axis=1, tiled=True)  68.7 us
    dot_general x14, matrix products, project(): return jnp.einsum(form, left, right, preferred_element_type=jnp.float32)  52.2 us
    gather x2, local copies, waits for them, and re-layouts, from_slots(): picked = buffer.reshape(slot_count, model_width)[target_slot]  20.4 us
    scatter x2, local copies, waits for them, and re-layouts, to_slots(): jnp.zeros((slot_count, model_width), jnp.bfloat16).at[target_slot]  17.9 us
  transfers between devices with their start and end apart: 4, of which 4 were waited for; matrix products, arithmetic and copies ran while one was open for 15% of the time, Pallas kernels for 0%

commit v1 on v0

v1 whole, which is shorter than its diff:
```python
import functools

import jax
import jax.numpy as jnp
from jax import lax
from jax.experimental import pallas as pl
from jax.experimental.pallas import tpu as pltpu
from jax.sharding import PartitionSpec as P

F32 = jnp.float32
BF16 = jnp.bfloat16
VMEM_LIMIT = 56 * 1024 * 1024
LANES = 128
ANY = pl.BlockSpec(memory_space=pl.ANY)


def dot(a, b):
    return jnp.dot(a, b, preferred_element_type=F32)


def dot_rows(a, b):
    return lax.dot_general(a, b, (((0,), (0,)), ((), ())), preferred_element_type=F32)


def dot_columns(a, b):
    return lax.dot_general(a, b, (((1,), (1,)), ((), ())), preferred_element_type=F32)


class Copies:
    def __init__(self, sems):
        self.sems, self.count = sems, 0

    def start(self, src, dst):
        copy = pltpu.make_async_copy(src, dst, self.sems.at[self.count])
        self.count += 1
        copy.start()
        return copy


def forward_kernel(cfg, own_ref, *refs):
    tok, width, ff, experts, cap, top_k, pieces = cfg
    blocks = refs[: len(pieces)]
    (wg, wu, dg, du, wd, dd) = refs[len(pieces) : len(pieces) + 6]
    outs = refs[len(pieces) + 6 :]
    (near_hbm, far_hbm, rows_hbm, sel_hbm, grad_hbm, hid_hbm) = outs[:6]
    (x, w, wdv, ddv, rows, sel, pre, grad, hid, out, part, sems) = outs[6:]
    copies = Copies(sems)
    n_blocks = sum(pieces) // tok
    per = n_blocks * cap
    at = 0
    x_in = []
    for piece, ref in zip(pieces, blocks):
        x_in.append((at // tok, copies.start(ref, x.at[pl.ds(at, piece)])))
        at += piece
    w_in, d_in = [], []
    for e in range(experts):
        w_in.append(
            [
                copies.start(src.at[e], w.at[e, :, pl.ds(k * ff, ff)])
                for k, src in enumerate((wg, wu, dg, du))
            ]
        )
        d_in.append([copies.start(wd.at[e], wdv.at[e]), copies.start(dd.at[e], ddv.at[e])])

    before = lax.broadcasted_iota(jnp.int32, (tok, tok), 0) < lax.broadcasted_iota(
        jnp.int32, (tok, tok), 1
    )
    before = before.astype(BF16)
    place = lax.broadcasted_iota(jnp.int32, (cap, tok), 0).astype(F32)
    weight = [[] for _ in range(experts)]
    waits = dict(x_in)
    for b in range(n_blocks):
        if b in waits:
            waits[b].wait()
        xb = x[b * tok : (b + 1) * tok, :]
        routes = xb[:, width : width + LANES].astype(F32).T
        ids = routes[0:top_k]
        gates = (routes[top_k : 2 * top_k] + routes[2 * top_k : 3 * top_k]) + routes[
            3 * top_k : 4 * top_k
        ]
        for e in range(experts):
            named = ids == (own_ref[0] + e).astype(F32)
            hit = jnp.sum(jnp.where(named, 1.0, 0.0), axis=0, keepdims=True)
            gate = jnp.sum(jnp.where(named, gates, 0.0), axis=0, keepdims=True)
            rank = dot(jnp.broadcast_to(hit, (8, tok)).astype(BF16), before)[0:1]
            chosen = jnp.where((rank == place) & (hit > 0.0), 1.0, 0.0)
            weight[e].append(jnp.sum(chosen * gate, axis=1, keepdims=True))
            sel[b, e * cap : (e + 1) * cap, :] = chosen.astype(BF16)
        picked = dot(sel[b], xb[:, 0:width]).astype(BF16)
        for e in range(experts):
            rows[e, b * cap : (b + 1) * cap, :] = picked[e * cap : (e + 1) * cap]
    done = [copies.start(rows, rows_hbm), copies.start(sel, sel_hbm)]

    step = 16
    for e in range(experts):
        for c in w_in[e]:
            c.wait()
        pre[e] = dot(rows[e], w[e])
    for e in range(experts):
        g_all = jnp.concatenate(weight[e], axis=0)
        for r in range(0, per, step):
            at = slice(r, r + step)
            g = g_all[at]
            p, u = pre[e, at, 0:ff], pre[e, at, ff : 2 * ff]
            dgv, duv = pre[e, at, 2 * ff : 3 * ff], pre[e, at, 3 * ff :]
            s = jax.nn.sigmoid(p)
            act = g * (p * s)
            slope = g * (s * (1.0 + p * (1.0 - s)))
            curv = g * (s * (1.0 - s) * (2.0 + p * (1.0 - 2.0 * s)))
            slope_up = slope * u
            grad[e, at, 0:ff] = slope_up
            grad[e, at, ff : 2 * ff] = curv * dgv * u + slope * duv
            grad[e, at, 2 * ff : 3 * ff] = act
            grad[e, at, 3 * ff :] = slope * dgv
            hid[e, at, 0:ff] = (act * u).astype(BF16)
            hid[e, at, ff:] = (slope_up * dgv + act * duv).astype(BF16)
        for c in d_in[e]:
            c.wait()
        h, hd = hid[e, :, 0:ff], hid[e, :, ff:]
        o = dot(h, wdv[e]).astype(BF16)
        od = (dot(hd, wdv[e]) + dot(h, ddv[e])).astype(BF16)
        for b in range(n_blocks):
            out[b, e * cap : (e + 1) * cap, 0:width] = o[b * cap : (b + 1) * cap]
            out[b, e * cap : (e + 1) * cap, width:] = od[b * cap : (b + 1) * cap]
    done += [copies.start(grad, grad_hbm), copies.start(hid, hid_hbm)]
    half = n_blocks // 2
    for b in [*range(half, n_blocks), *range(half)]:
        part[b * tok : (b + 1) * tok, :] = dot_rows(sel[b], out[b]).astype(BF16)
        if b == n_blocks - 1:
            done.append(copies.start(part.at[pl.ds(half * tok, half * tok)], far_hbm))
        if b == half - 1:
            done.append(copies.start(part.at[pl.ds(0, half * tok)], near_hbm))
    for c in done:
        c.wait()


def forward(own, pieces, weights, tok, cap, top_k):
    wg, _, wd = weights[0], weights[1], weights[4]
    experts, width, ff = wg.shape
    sizes = tuple(p.shape[0] for p in pieces)
    total = sum(sizes)
    n_blocks = total // tok
    per = n_blocks * cap
    shape = jax.ShapeDtypeStruct
    return pl.pallas_call(
        functools.partial(forward_kernel, (tok, width, ff, experts, cap, top_k, sizes)),
        in_specs=[pl.BlockSpec(memory_space=pltpu.SMEM)] + [ANY] * (len(pieces) + 6),
        out_specs=[ANY] * 6,
        out_shape=[
            shape((total // 2, 2 * width), BF16),
            shape((total // 2, 2 * width), BF16),
            shape((experts, per, width), BF16),
            shape((n_blocks, experts * cap, tok), BF16),
            shape((experts, per, 4 * ff), F32),
            shape((experts, per, 2 * ff), BF16),
        ],
        scratch_shapes=[
            pltpu.VMEM((total, pieces[0].shape[1]), BF16),
            pltpu.VMEM((experts, width, 4 * ff), BF16),
            pltpu.VMEM((experts, ff, width), BF16),
            pltpu.VMEM((experts, ff, width), BF16),
            pltpu.VMEM((experts, per, width), BF16),
            pltpu.VMEM((n_blocks, experts * cap, tok), BF16),
            pltpu.VMEM((experts, per, 4 * ff), F32),
            pltpu.VMEM((experts, per, 4 * ff), F32),
            pltpu.VMEM((experts, per, 2 * ff), BF16),
            pltpu.VMEM((n_blocks, experts * cap, 2 * width), BF16),
            pltpu.VMEM((total, 2 * width), BF16),
            pltpu.SemaphoreType.DMA((len(pieces) + 6 * experts + 6,)),
        ],
        compiler_params=pltpu.CompilerParams(vmem_limit_bytes=VMEM_LIMIT),
        cost_estimate=pl.CostEstimate(
            flops=2 * experts * per * width * (7 * ff + 3 * tok),
            bytes_accessed=2 * total * 3 * width + 12 * experts * width * ff,
            transcendentals=experts * per * ff,
        ),
    )(own, *pieces, *weights)


def backward_kernel(cfg, *refs):
    tok, width, ff, experts, cap, sizes, quarters, last = cfg
    refs = list(refs)
    take = lambda k: [refs.pop(0) for _ in range(k)]
    pieces = [take(len(sizes)) for _ in range(quarters)]
    saved = [take(4) for _ in range(quarters)]
    wd, dd = take(2)
    if last:
        in_gu, in_d = take(2)
        gate_hbm, up_hbm, down_hbm = take(3)
    else:
        out_gu, out_d = take(2)
    (rm, sel, grad, hid, rows, wdv, ddv, got, gud, acc_gu, acc_d) = take(11)
    if last:
        gate, up, down = take(3)
    (sems,) = take(1)
    copies = Copies(sems)
    n_blocks = sum(sizes) // tok
    per = n_blocks * cap

    def load(q):
        slot = q % 2
        rows_hbm, sel_hbm, grad_hbm, hid_hbm = saved[q]
        at, started = 0, []
        started.append(copies.start(sel_hbm, sel.at[slot]))
        for size, ref in zip(sizes, pieces[q]):
            started.append(copies.start(ref, rm.at[slot, pl.ds(at, size)]))
            at += size
        started.append(copies.start(grad_hbm, grad.at[slot]))
        for e in range(experts):
            where = pl.ds(q * per, per)
            started.append(copies.start(hid_hbm.at[e], hid.at[e, where]))
            started.append(copies.start(rows_hbm.at[e], rows.at[e, where]))
        return started

    waiting = [load(0)]
    weights = [copies.start(wd, wdv), copies.start(dd, ddv)]
    if last:
        acc_in = [copies.start(in_gu, acc_gu), copies.start(in_d, acc_d)]
    step = 16
    for q in range(quarters):
        slot = q % 2
        if q + 1 < quarters:
            waiting.append(load(q + 1))
        for c in waiting[q]:
            c.wait()
        if q == 0:
            for c in weights:
                c.wait()
        for b in range(n_blocks):
            picked = dot(sel[slot, b], rm[slot, b * tok : (b + 1) * tok, :]).astype(BF16)
            for e in range(experts):
                at = q * per + b * cap
                got[e, at : at + cap, :] = picked[e * cap : (e + 1) * cap]
        for e in range(experts):
            r = got[e, q * per : (q + 1) * per, 0:width]
            m = got[e, q * per : (q + 1) * per, width:]
            grad_h = dot_columns(r, wdv[e])
            grad_d = dot_columns(m, wdv[e]) + dot_columns(r, ddv[e])
            for k in range(0, per, step):
                at = slice(k, k + step)
                to = slice(q * per + k, q * per + k + step)
                gh, gd = grad_h[at], grad_d[at]
                part = lambda i: grad[slot, e, at, i * ff : (i + 1) * ff]
                gud[e, to, 0:ff] = (gd * part(0) + gh * part(1)).astype(BF16)
                gud[e, to, ff:] = (gd * part(2) + gh * part(3)).astype(BF16)

    done = []
    if last:
        for c in acc_in:
            c.wait()
    for e in range(experts):
        gu = dot_rows(rows[e], gud[e])
        if last:
            gu = (gu + acc_gu[e]).astype(BF16)
            gate[e] = gu[:, 0:ff]
            up[e] = gu[:, ff:]
            done.append(copies.start(gate.at[e], gate_hbm.at[e]))
            done.append(copies.start(up.at[e], up_hbm.at[e]))
        else:
            acc_gu[e] = gu
            done.append(copies.start(acc_gu.at[e], out_gu.at[e]))
        d = dot_rows(hid[e, :, ff:], got[e, :, 0:width])
        d += dot_rows(hid[e, :, 0:ff], got[e, :, width:])
        if last:
            down[e] = (d + acc_d[e]).astype(BF16)
            done.append(copies.start(down.at[e], down_hbm.at[e]))
        else:
            acc_d[e] = d
            done.append(copies.start(acc_d.at[e], out_d.at[e]))
    for c in done:
        c.wait()


def backward(quarters, wd, dd, tok, cap, acc=None):
    experts, ff, width = wd.shape
    count = len(quarters)
    last = acc is not None
    sizes = tuple(p.shape[0] for p in quarters[0][0])
    total = sum(sizes)
    n_blocks = total // tok
    per = n_blocks * cap
    shape = jax.ShapeDtypeStruct
    operands = [p for q in quarters for p in q[0]] + [s for q in quarters for s in q[1]] + [wd, dd]
    gu, d = (experts, width, 2 * ff), (experts, ff, width)
    if last:
        operands += list(acc)
        outs = [shape((experts, width, ff), BF16)] * 2 + [shape(d, BF16)]
    else:
        outs = [shape(gu, F32), shape(d, F32)]
    scratch = [
        pltpu.VMEM((2, total, 2 * width), BF16),
        pltpu.VMEM((2, n_blocks, experts * cap, tok), BF16),
        pltpu.VMEM((2, experts, per, 4 * ff), F32),
        pltpu.VMEM((experts, count * per, 2 * ff), BF16),
        pltpu.VMEM((experts, count * per, width), BF16),
        pltpu.VMEM(d, BF16),
        pltpu.VMEM(d, BF16),
        pltpu.VMEM((experts, count * per, 2 * width), BF16),
        pltpu.VMEM((experts, count * per, 2 * ff), BF16),
        pltpu.VMEM(gu, F32),
        pltpu.VMEM(d, F32),
    ]
    if last:
        scratch += [pltpu.VMEM(o.shape, BF16) for o in outs]
    n_sems = count * (len(sizes) + 2 + 2 * experts) + 4 + 3 * experts
    return pl.pallas_call(
        functools.partial(
            backward_kernel, (tok, width, ff, experts, cap, sizes, count, last)
        ),
        in_specs=[ANY] * len(operands),
        out_specs=[ANY] * len(outs),
        out_shape=outs,
        scratch_shapes=scratch + [pltpu.SemaphoreType.DMA((n_sems,))],
        compiler_params=pltpu.CompilerParams(vmem_limit_bytes=VMEM_LIMIT),
        cost_estimate=pl.CostEstimate(
            flops=2 * experts * count * per * width * (7 * ff + 2 * tok),
            bytes_accessed=2 * count * total * 3 * width + 12 * experts * width * ff,
            transcendentals=0,
        ),
    )(*operands)


def local(
    tokens, target, expert_ids, gate_weights, w_gate, w_up, w_down, dir_gate, dir_up, dir_down
):
    n = lax.axis_size("expert")
    me = lax.axis_index("expert")
    nz = n // 4
    experts, width, ff = w_gate.shape
    tok, top_k = expert_ids.shape
    capacity = max(2, 3 * tok * top_k // (2 * experts * n))
    cap = -(-capacity // 16) * 16

    def send(x, to):
        return lax.ppermute(x, "expert", [(i, to(i)) for i in range(n)])

    ahead = lambda x: send(x, lambda i: (i + 4) % n)
    side = lambda x: send(x, lambda i: i ^ 2)
    core = lambda x: send(x, lambda i: i ^ 1)

    def add(a, b):
        return a.astype(F32) + b.astype(F32)

    def gather(x):
        quarters = []
        a = x
        for d in range(nz):
            if d:
                a = ahead(a)
            b = side(a)
            quarters.append((a, b, core(a), core(b)))
        return quarters

    def scatter_sum(parts):
        def plane(near, far):
            got = core(far)
            s = add(near[tok:], got[tok:]).astype(BF16)
            return add(add(near[0:tok], got[0:tok]), side(s))

        total = None
        for d in [*range(1, nz), 0]:
            s = plane(*parts[d])
            total = s if total is None else s + ahead(total.astype(BF16)).astype(F32)
        return total

    exact = lambda a: lax.reduce_precision(a, 8, 7)
    high = exact(gate_weights)
    middle = exact(gate_weights - high)
    low = gate_weights - high - middle
    routes = jnp.concatenate([expert_ids.astype(F32), high, middle, low], 1).astype(BF16)
    routes = jnp.pad(routes, ((0, 0), (0, LANES - 4 * top_k)))
    own = (me * experts).astype(jnp.int32).reshape(1)
    weights = (w_gate, w_up, dir_gate, dir_up, w_down, dir_down)

    x = gather(jnp.concatenate([tokens, routes], 1))
    parts, saved = [], []
    for d in range(nz):
        near, far, *rest = forward(own, x[d], weights, tok, cap, top_k)
        parts.append((near, far))
        saved.append(rest)
    total = scatter_sum(parts)
    total = jnp.concatenate([total[:, 0:width] - target.astype(F32), total[:, width:]], 1)
    rm = gather(total.astype(BF16))
    quarters = list(zip(rm, saved))
    acc = backward(quarters[:-1], w_down, dir_down, tok, cap)
    return tuple(backward(quarters[-1:], w_down, dir_down, tok, cap, acc=acc))


def solution(mesh):
    in_specs = (
        P(("groups", "expert"), None),
        P(("groups", "expert"), None),
        P(("groups", "expert"), None),
        P(("groups", "expert"), None),
        P("expert", None, None),
        P("expert", None, None),
        P("expert", None, None),
        P("expert", None, None),
        P("expert", None, None),
        P("expert", None, None),
    )
    out_specs = (
        P(("groups", "expert"), None, None),
        P(("groups", "expert"), None, None),
        P(("groups", "expert"), None, None),
    )
    return jax.shard_map(local, mesh=mesh, in_specs=in_specs, out_specs=out_specs, check_vma=False)
```

time: 620 us -> 294 us (0.47)
  the two profiles are of different devices: /device:TPU:13 before, /device:TPU:1 now
where the time goes in v1:
time: 294 us; the launch traced here: 289 us
  waiting for transfers between devices  112 us (38%)
  Pallas kernels  80.2 us (27%)
  starting transfers between devices  79.8 us (27%)
  other arithmetic  11.4 us (4%)
  local copies, waits for them, and re-layouts  4.41 us (2%)
    ppermute x41, waiting for transfers between devices, send(): return lax.ppermute(x, 'expert', [(i, to(i)) for i in range(n)])  112 us
    ppermute x41, starting transfers between devices, send(): return lax.ppermute(x, 'expert', [(i, to(i)) for i in range(n)])  79.8 us
    pallas_call x4, Pallas kernels, forward(): pl.pallas_call(functools.partial(forward_kernel, (tok, width, ff, experts...  44.3 us
    pallas_call x2, Pallas kernels, backward(): pl.pallas_call(functools.partial(backward_kernel, (tok, width, ff, expert...  35.9 us
  transfers between devices with their start and end apart: 41, of which 18 were waited for; matrix products, arithmetic and copies ran while one was open for 3% of the time, Pallas kernels for 23%

profile of v1, /device:TPU:1, one launch (start us, length us, event | category | flops | bytes accessed | tf_op | source)
XLA Modules:
  0.0 289.0 jit_solution(2448424396161582974)
XLA Ops:
  2.1 1.0 fusion.2.refs_0_
  3.2 2.2 collective-permute-start.5
  5.4 11.6 %collective-permute-done.5.refs_0_ = bf16[128,1664]{1,0:T(8,128)(2,1)S(1)} collective-permute-done((bf16[128,1664]{1,0:T(8,128)(2,1)S(1)}, bf16[128,1664]{1,0:T(8,128)(2,1)S(1)}, u32[]{:S(2)}, u32[]{:S(2)}) %collective-permute-start.5) | collective-permute-done | bytes 426016 | tf_op jit(solution)/shard_map/ppermute | solution.py:335
  16.9 1.0 collective-permute-start.18
  17.9 1.8 collective-permute-start.19
  19.7 7.3 %collective-permute-done.18.refs_1_ = bf16[128,1664]{1,0:T(8,128)(2,1)S(1)} collective-permute-done((bf16[128,1664]{1,0:T(8,128)(2,1)S(1)}, bf16[128,1664]{1,0:T(8,128)(2,1)S(1)}, u32[]{:S(2)}, u32[]{:S(2)}) %collective-permute-start.18) | collective-permute-done | bytes 426016 | tf_op jit(solution)/shard_map/ppermute | solution.py:335
  27.0 2.1 collective-permute-start.20
  31.3 11.1 %shard_map.124 = (bf16[256,3072]{1,0:T(8,128)(2,1)}, bf16[256,3072]{1,0:T(8,128)(2,1)}, bf16[2,192,1536]{2,1,0:T(8,128)(2,1)}, bf16[4,96,128]{2,1,0:T(8,128)(2,1...) custom-call(s32[1]{0:T(128)} %bitcast.own_ref, bf16[128,1664]{1,0:T(8,128)(2,1)} %copy-done.12, ...), custom_call_target="tpu_custom_call" | custom-call | flops 3623878656 | bytes 18874368 | tf_op jit(solution)/shard_map/pallas_call | solution.py:145
  42.4 2.4 collective-permute-start.21
  45.6 2.7 collective-permute-done.14.refs_2_
  49.8 11.1 %shard_map.123 = (bf16[256,3072]{1,0:T(8,128)(2,1)}, bf16[256,3072]{1,0:T(8,128)(2,1)}, bf16[2,192,1536]{2,1,0:T(8,128)(2,1)}, bf16[4,96,128]{2,1,0:T(8,128)(2,1...) custom-call(s32[1]{0:T(128)} %bitcast.own_ref, bf16[128,1664]{1,0:T(8,128)(2,1)} %copy-done.11, ...), custom_call_target="tpu_custom_call" | custom-call | flops 3623878656 | bytes 18874368 | tf_op jit(solution)/shard_map/pallas_call | solution.py:145
  61.1 1.0 collective-permute-start
  62.6 0.9 collective-permute-start.1
  63.5 8.6 %collective-permute-done.refs_1_ = bf16[128,1664]{1,0:T(8,128)(2,1)S(1)} collective-permute-done((bf16[128,1664]{1,0:T(8,128)(2,1)S(1)}, bf16[128,1664]{1,0:T(8,128)(2,1)S(1)}, u32[]{:S(2)}, u32[]{:S(2)}) %collective-permute-start) | collective-permute-done | bytes 426016 | tf_op jit(solution)/shard_map/ppermute | solution.py:335
  72.2 2.0 collective-permute-start.2
  74.2 7.1 %collective-permute-done.8.refs_1_ = bf16[128,1664]{1,0:T(8,128)(2,1)S(1)} collective-permute-done((bf16[128,1664]{1,0:T(8,128)(2,1)}, bf16[128,1664]{1,0:T(8,128)(2,1)S(1)}, u32[]{:S(2)}, u32[]{:S(2)}) %collective-permute-start.8) | collective-permute-done | bytes 426016 | tf_op jit(solution)/shard_map/ppermute | solution.py:335
  81.3 1.2 collective-permute-start.9
  82.6 1.1 add_convert_fusion.3
  84.2 1.0 collective-permute-start.22
  85.2 11.1 %shard_map.122 = (bf16[256,3072]{1,0:T(8,128)(2,1)}, bf16[256,3072]{1,0:T(8,128)(2,1)}, bf16[2,192,1536]{2,1,0:T(8,128)(2,1)}, bf16[4,96,128]{2,1,0:T(8,128)(2,1...) custom-call(s32[1]{0:T(128)} %bitcast.own_ref, bf16[128,1664]{1,0:T(8,128)(2,1)} %collective-permute-done.7.refs_0_, ...), custom_call_target="tpu_custom_call" | custom-call | flops 3623878656 | bytes 18874368 | tf_op jit(solution)/shard_map/pallas_call | solution.py:145
  97.8 5.5 %collective-permute-done.22 = bf16[128,3072]{1,0:T(8,128)(2,1)} collective-permute-done((bf16[128,3072]{1,0:T(8,128)(2,1)}, bf16[128,3072]{1,0:T(8,128)(2,1)}, u32[]{:S(2)}, u32[]{:S(2)}) %collective-permute-start.22) | collective-permute-done | bytes 786464 | tf_op jit(solution)/shard_map/ppermute | solution.py:335
  103.3 2.4 add_convert_fusion.2
  106.2 11.1 %shard_map.121 = (bf16[256,3072]{1,0:T(8,128)(2,1)}, bf16[256,3072]{1,0:T(8,128)(2,1)}, bf16[2,192,1536]{2,1,0:T(8,128)(2,1)}, bf16[4,96,128]{2,1,0:T(8,128)(2,1...) custom-call(s32[1]{0:T(128)} %bitcast.own_ref, bf16[128,1664]{1,0:T(8,128)(2,1)} %copy-done, ...), custom_call_target="tpu_custom_call" | custom-call | flops 3623878656 | bytes 18874368 | tf_op jit(solution)/shard_map/pallas_call | solution.py:145
  117.3 2.1 collective-permute-start.3
  119.4 1.3 add_convert_fusion.5
  120.7 1.0 collective-permute-start.12
  121.8 3.4 %collective-permute-done.23 = bf16[128,3072]{1,0:T(8,128)(2,1)S(1)} collective-permute-done((bf16[128,3072]{1,0:T(8,128)(2,1)}, bf16[128,3072]{1,0:T(8,128)(2,1)S(1)}, u32[]{:S(2)}, u32[]{:S(2)}) %collective-permute-start.23) | collective-permute-done | bytes 786464 | tf_op jit(solution)/shard_map/ppermute | solution.py:335
  125.2 1.6 add_convert_fusion.1
  127.1 1.0 collective-permute-start.4
  128.2 11.8 %collective-permute-done.12 = bf16[128,3072]{1,0:T(8,128)(2,1)S(1)} collective-permute-done((bf16[128,3072]{1,0:T(8,128)(2,1)S(1)}, bf16[128,3072]{1,0:T(8,128)(2,1)S(1)}, u32[]{:S(2)}, u32[]{:S(2)}) %collective-permute-start.12) | collective-permute-done | bytes 786464 | tf_op jit(solution)/shard_map/ppermute | solution.py:335
  140.0 4.9 %collective-permute-done.24 = bf16[128,3072]{1,0:T(8,128)(2,1)S(1)} collective-permute-done((bf16[128,3072]{1,0:T(8,128)(2,1)S(1)}, bf16[128,3072]{1,0:T(8,128)(2,1)S(1)}, u32[]{:S(2)}, u32[]{:S(2)}) %collective-permute-start.24) | collective-permute-done | bytes 786464 | tf_op jit(solution)/shard_map/ppermute | solution.py:335
  144.8 1.6 add_convert_fusion
  146.5 10.3 %collective-permute-done.4 = bf16[128,3072]{1,0:T(8,128)(2,1)S(1)} collective-permute-done((bf16[128,3072]{1,0:T(8,128)(2,1)S(1)}, bf16[128,3072]{1,0:T(8,128)(2,1)S(1)}, u32[]{:S(2)}, u32[]{:S(2)}) %collective-permute-start.4) | collective-permute-done | bytes 786464 | tf_op jit(solution)/shard_map/ppermute | solution.py:335
  156.8 6.7 %collective-permute-done.25 = bf16[128,3072]{1,0:T(8,128)(2,1)S(1)} collective-permute-done((bf16[128,3072]{1,0:T(8,128)(2,1)S(1)}, bf16[128,3072]{1,0:T(8,128)(2,1)S(1)}, u32[]{:S(2)}, u32[]{:S(2)}) %collective-permute-start.25) | collective-permute-done | bytes 786464 | tf_op jit(solution)/shard_map/ppermute | solution.py:335
  164.3 1.0 collective-permute-start.32
  165.3 15.0 %collective-permute-done.26.refs_4_ = bf16[128,3072]{1,0:T(8,128)(2,1)S(1)} collective-permute-done((bf16[128,3072]{1,0:T(8,128)(2,1)S(1)}, bf16[128,3072]{1,0:T(8,128)(2,1)S(1)}, u32[]{:S(2)}, u32[]{:S(2)}) %collective-permute-start.26) | collective-permute-done | bytes 786464 | tf_op jit(solution)/shard_map/ppermute | solution.py:335
  180.3 6.4 %collective-permute-start.33 = (bf16[128,3072]{1,0:T(8,128)(2,1)S(1)}, bf16[128,3072]{1,0:T(8,128)(2,1)S(1)}, u32[]{:S(2)}, u32[]{:S(2)}) collective-permute-start(bf16[128,3072]{1,0:T(8,128)(2,1)S(1)} %pad_maximum_fusion.refs_0_), channel_id=1, source_target_pairs={{0,1},{1,0},{2,3},{3,2},{4,5},{5,4},{6,7},{7,6},{8,9},{9,8},{10,11... | collective-permute-start | bytes 2359304 | tf_op jit(solution)/shard_map/ppermute | solution.py:335
  186.8 9.5 %collective-permute-done.27.refs_8_ = bf16[128,3072]{1,0:T(8,128)(2,1)S(1)} collective-permute-done((bf16[128,3072]{1,0:T(8,128)(2,1)S(1)}, bf16[128,3072]{1,0:T(8,128)(2,1)S(1)}, u32[]{:S(2)}, u32[]{:S(2)}) %collective-permute-start.27) | collective-permute-done | bytes 786464 | tf_op jit(solution)/shard_map/ppermute | solution.py:335
  196.5 1.0 collective-permute-start.35
  198.0 8.5 %collective-permute-start.36 = (bf16[128,3072]{1,0:T(8,128)(2,1)S(1)}, bf16[128,3072]{1,0:T(8,128)(2,1)}, u32[]{:S(2)}, u32[]{:S(2)}) collective-permute-start(bf16[128,3072]{1,0:T(8,128)(2,1)S(1)} %collective-permute-done.26.refs_4_), channel_id=1, source_target_pairs={{0,1},{1,0},{2,3},{3,2},{4,5},{5,4},{6,7},{7,6},{8,9},{9,8},{10,11... | collective-permute-start | bytes 2359304 | tf_op jit(solution)/shard_map/ppermute | solution.py:335
  206.6 5.7 %collective-permute-done.28.refs_0_ = bf16[128,3072]{1,0:T(8,128)(2,1)S(1)} collective-permute-done((bf16[128,3072]{1,0:T(8,128)(2,1)S(1)}, bf16[128,3072]{1,0:T(8,128)(2,1)S(1)}, u32[]{:S(2)}, u32[]{:S(2)}) %collective-permute-start.28) | collective-permute-done | bytes 786464 | tf_op jit(solution)/shard_map/ppermute | solution.py:335
  212.3 1.0 collective-permute-start.29
  213.3 11.7 %collective-permute-start.37 = (bf16[128,3072]{1,0:T(8,128)(2,1)S(1)}, bf16[128,3072]{1,0:T(8,128)(2,1)S(1)}, u32[]{:S(2)}, u32[]{:S(2)}) collective-permute-start(bf16[128,3072]{1,0:T(8,128)(2,1)S(1)} %collective-permute-done.35.refs_5_), channel_id=1, source_target_pairs={{0,1},{1,0},{2,3},{3,2},{4,5},{5,4},{6,7},{7,6},{8,9},{9,8},{10,11... | collective-permute-start | bytes 2359304 | tf_op jit(solution)/shard_map/ppermute | solution.py:335
  225.0 16.8 %collective-permute-start.40 = (bf16[128,3072]{1,0:T(8,128)(2,1)S(1)}, bf16[128,3072]{1,0:T(8,128)(2,1)S(1)}, u32[]{:S(2)}, u32[]{:S(2)}) collective-permute-start(bf16[128,3072]{1,0:T(8,128)(2,1)S(1)} %collective-permute-done.38.refs_9_), channel_id=1, source_target_pairs={{0,1},{1,0},{2,3},{3,2},{4,5},{5,4},{6,7},{7,6},{8,9},{9,8},{10,11... | collective-permute-start | bytes 2359304 | tf_op jit(solution)/shard_map/ppermute | solution.py:335
  241.9 8.3 %collective-permute-start.31 = (bf16[128,3072]{1,0:T(8,128)(2,1)S(1)}, bf16[128,3072]{1,0:T(8,128)(2,1)S(1)}, u32[]{:S(2)}, u32[]{:S(2)}) collective-permute-start(bf16[128,3072]{1,0:T(8,128)(2,1)S(1)} %collective-permute-done.29.refs_1_), channel_id=1, source_target_pairs={{0,1},{1,0},{2,3},{3,2},{4,5},{5,4},{6,7},{7,6},{8,9},{9,8},{10,11... | collective-permute-start | bytes 2359304 | tf_op jit(solution)/shard_map/ppermute | solution.py:335
  250.3 0.9 copy-done.28
  251.7 23.4 %shard_map.125 = (f32[2,1536,768]{2,1,0:T(8,128)}, f32[2,384,1536]{2,1,0:T(8,128)}) custom-call(bf16[128,3072]{1,0:T(8,128)(2,1)} %copy-done.9, bf16[128,3072]{1,0:T(8,128)(2,1)} %copy-done.22, bf16[128,3072]{1,0:T(8,128)(2,1)} %copy-done.24, bf16[128,3072]{1,0:T(8,128)(2,1)} %copy-done.25, bf16[128,3072]{1,0:T(8,128)(2,1)} %copy-done.21, ...), custom_call_target="tpu_custom_call" | custom-call | flops 10418651136 | bytes 28311552 | tf_op jit(solution)/shard_map/pallas_call | solution.py:306
  276.2 12.5 %shard_map.126 = (bf16[2,1536,384]{2,1,0:T(8,128)(2,1)}, bf16[2,1536,384]{2,1,0:T(8,128)(2,1)}, bf16[2,384,1536]{2,1,0:T(8,128)(2,1)}) custom-call(bf16[128,3072]{1,0:T(8,128)(2,1)} %copy-done.5, bf16[128,3072]{1,0:T(8,128)(2,1)} %copy-done.6, bf16[128,3072]{1,0:T(8,128)(2,1)} %copy-done.7, bf16[128,3072]{1,0:T(8,128)(2,1)} %copy-done.8, ...), custom_call_target="tpu_custom_call" | custom-call | flops 3472883712 | bytes 18874368 | tf_op jit(solution)/shard_map/pallas_call | solution.py:306
  (118 shorter events, 12.9 us)
Async XLA Ops:
  3.2 59.4 %copy-start = (bf16[128,1664]{1,0:T(8,128)(2,1)}, bf16[128,1664]{1,0:T(8,128)(2,1)S(1)}, u32[]{:S(2)}) copy-start(bf16[128,1664]{1,0:T(8,128)(2,1)S(1)} %fusion.2.refs_0_) | copy-start | bytes 1277956
  3.2 13.7 %collective-permute-start.5 = (bf16[128,1664]{1,0:T(8,128)(2,1)S(1)}, bf16[128,1664]{1,0:T(8,128)(2,1)S(1)}, u32[]{:S(2)}, u32[]{:S(2)}) collective-permute-start(bf16[128,1664]{1,0:T(8,128)(2,1)S(1)} %fusion.2.refs_0_), channel_id=1, source_target_pairs={{0,4},{1,5},{2,6},{3,7},{4,8},{5,9},{6,10},{7,11},{8,12},{9,13},{1... | collective-permute-start | bytes 1277960 | tf_op jit(solution)/shard_map/ppermute | solution.py:335
  16.9 10.1 %collective-permute-start.18 = (bf16[128,1664]{1,0:T(8,128)(2,1)S(1)}, bf16[128,1664]{1,0:T(8,128)(2,1)S(1)}, u32[]{:S(2)}, u32[]{:S(2)}) collective-permute-start(bf16[128,1664]{1,0:T(8,128)(2,1)S(1)} %collective-permute-done.5.refs_0_), channel_id=1, source_target_pairs={{0,2},{1,3},{2,0},{3,1},{4,6},{5,7},{6,4},{7,5},{8,10},{9,11},{10,... | collective-permute-start | bytes 1277960 | tf_op jit(solution)/shard_map/ppermute | solution.py:335
  17.9 11.4 %collective-permute-start.6 = (bf16[128,1664]{1,0:T(8,128)(2,1)S(1)}, bf16[128,1664]{1,0:T(8,128)(2,1)S(1)}, u32[]{:S(2)}, u32[]{:S(2)}) collective-permute-start(bf16[128,1664]{1,0:T(8,128)(2,1)S(1)} %collective-permute-done.5.refs_0_), channel_id=1, source_target_pairs={{0,4},{1,5},{2,6},{3,7},{4,8},{5,9},{6,10},{7,11},{8,12},{9,13},{1... | collective-permute-start | bytes 1277960 | tf_op jit(solution)/shard_map/ppermute | solution.py:335
  17.9 12.2 %collective-permute-start.19 = (bf16[128,1664]{1,0:T(8,128)(2,1)S(1)}, bf16[128,1664]{1,0:T(8,128)(2,1)S(1)}, u32[]{:S(2)}, u32[]{:S(2)}) collective-permute-start(bf16[128,1664]{1,0:T(8,128)(2,1)S(1)} %collective-permute-done.5.refs_0_), channel_id=1, source_target_pairs={{0,1},{1,0},{2,3},{3,2},{4,5},{5,4},{6,7},{7,6},{8,9},{9,8},{10,11... | collective-permute-start | bytes 1277960 | tf_op jit(solution)/shard_map/ppermute | solution.py:335
  27.0 3.5 %collective-permute-start.20 = (bf16[128,1664]{1,0:T(8,128)(2,1)S(1)}, bf16[128,1664]{1,0:T(8,128)(2,1)S(1)}, u32[]{:S(2)}, u32[]{:S(2)}) collective-permute-start(bf16[128,1664]{1,0:T(8,128)(2,1)S(1)} %collective-permute-done.18.refs_1_), channel_id=1, source_target_pairs={{0,1},{1,0},{2,3},{3,2},{4,5},{5,4},{6,7},{7,6},{8,9},{9,8},{10,11... | collective-permute-start | bytes 1277960 | tf_op jit(solution)/shard_map/ppermute | solution.py:335
  29.3 15.6 %collective-permute-start.13 = (bf16[128,1664]{1,0:T(8,128)(2,1)S(1)}, bf16[128,1664]{1,0:T(8,128)(2,1)S(1)}, u32[]{:S(2)}, u32[]{:S(2)}) collective-permute-start(bf16[128,1664]{1,0:T(8,128)(2,1)S(1)} %collective-permute-done.6.refs_0_), channel_id=1, source_target_pairs={{0,2},{1,3},{2,0},{3,1},{4,6},{5,7},{6,4},{7,5},{8,10},{9,11},{10,... | collective-permute-start | bytes 1277960 | tf_op jit(solution)/shard_map/ppermute | solution.py:335
  42.4 40.1 %collective-permute-start.21 = (bf16[256,3072]{1,0:T(8,128)(2,1)}, bf16[256,3072]{1,0:T(8,128)(2,1)S(1)}, u32[]{:S(2)}, u32[]{:S(2)}) collective-permute-start(bf16[256,3072]{1,0:T(8,128)(2,1)} %get-tuple-element.36), channel_id=1, source_target_pairs={{0,1},{1,0},{2,3},{3,2},{4,5},{5,4},{6,7},{7,6},{8,9},{9,8},{10,11... | collective-permute-start | bytes 4718600 | tf_op jit(solution)/shard_map/ppermute | solution.py:335
  44.8 3.5 %collective-permute-start.14 = (bf16[128,1664]{1,0:T(8,128)(2,1)S(1)}, bf16[128,1664]{1,0:T(8,128)(2,1)S(1)}, u32[]{:S(2)}, u32[]{:S(2)}) collective-permute-start(bf16[128,1664]{1,0:T(8,128)(2,1)S(1)} %collective-permute-done.6.refs_0_), channel_id=1, source_target_pairs={{0,1},{1,0},{2,3},{3,2},{4,5},{5,4},{6,7},{7,6},{8,9},{9,8},{10,11... | collective-permute-start | bytes 1277960 | tf_op jit(solution)/shard_map/ppermute | solution.py:335
  44.9 4.0 %collective-permute-start.15 = (bf16[128,1664]{1,0:T(8,128)(2,1)S(1)}, bf16[128,1664]{1,0:T(8,128)(2,1)S(1)}, u32[]{:S(2)}, u32[]{:S(2)}) collective-permute-start(bf16[128,1664]{1,0:T(8,128)(2,1)S(1)} %collective-permute-done.13.refs_1_), channel_id=1, source_target_pairs={{0,1},{1,0},{2,3},{3,2},{4,5},{5,4},{6,7},{7,6},{8,9},{9,8},{10,11... | collective-permute-start | bytes 1277960 | tf_op jit(solution)/shard_map/ppermute | solution.py:335
  45.3 16.8 %collective-permute-start.7 = (bf16[128,1664]{1,0:T(8,128)(2,1)S(1)}, bf16[128,1664]{1,0:T(8,128)(2,1)}, u32[]{:S(2)}, u32[]{:S(2)}) collective-permute-start(bf16[128,1664]{1,0:T(8,128)(2,1)S(1)} %collective-permute-done.6.refs_0_), channel_id=1, source_target_pairs={{0,4},{1,5},{2,6},{3,7},{4,8},{5,9},{6,10},{7,11},{8,12},{9,13},{1... | collective-permute-start | bytes 1277960 | tf_op jit(solution)/shard_map/ppermute | solution.py:335
  60.9 36.1 %collective-permute-start.16 = (bf16[256,3072]{1,0:T(8,128)(2,1)}, bf16[256,3072]{1,0:T(8,128)(2,1)S(1)}, u32[]{:S(2)}, u32[]{:S(2)}) collective-permute-start(bf16[256,3072]{1,0:T(8,128)(2,1)} %get-tuple-element.34), channel_id=1, source_target_pairs={{0,1},{1,0},{2,3},{3,2},{4,5},{5,4},{6,7},{7,6},{8,9},{9,8},{10,11... | collective-permute-start | bytes 4718600 | tf_op jit(solution)/shard_map/ppermute | solution.py:335
  61.1 11.0 %collective-permute-start = (bf16[128,1664]{1,0:T(8,128)(2,1)S(1)}, bf16[128,1664]{1,0:T(8,128)(2,1)S(1)}, u32[]{:S(2)}, u32[]{:S(2)}) collective-permute-start(bf16[128,1664]{1,0:T(8,128)(2,1)S(1)} %fusion.2.refs_0_), channel_id=1, source_target_pairs={{0,2},{1,3},{2,0},{3,1},{4,6},{5,7},{6,4},{7,5},{8,10},{9,11},{10,... | collective-permute-start | bytes 1277960 | tf_op jit(solution)/shard_map/ppermute | solution.py:335
  62.1 19.2 %collective-permute-start.8 = (bf16[128,1664]{1,0:T(8,128)(2,1)}, bf16[128,1664]{1,0:T(8,128)(2,1)S(1)}, u32[]{:S(2)}, u32[]{:S(2)}) collective-permute-start(bf16[128,1664]{1,0:T(8,128)(2,1)} %collective-permute-done.7.refs_0_), channel_id=1, source_target_pairs={{0,2},{1,3},{2,0},{3,1},{4,6},{5,7},{6,4},{7,5},{8,10},{9,11},{10,... | collective-permute-start | bytes 1277960 | tf_op jit(solution)/shard_map/ppermute | solution.py:335
  62.6 43.6 %collective-permute-start.1 = (bf16[128,1664]{1,0:T(8,128)(2,1)S(1)}, bf16[128,1664]{1,0:T(8,128)(2,1)}, u32[]{:S(2)}, u32[]{:S(2)}) collective-permute-start(bf16[128,1664]{1,0:T(8,128)(2,1)S(1)} %fusion.2.refs_0_), channel_id=1, source_target_pairs={{0,1},{1,0},{2,3},{3,2},{4,5},{5,4},{6,7},{7,6},{8,9},{9,8},{10,11... | collective-permute-start | bytes 1277960 | tf_op jit(solution)/shard_map/ppermute | solution.py:335
  72.2 34.1 %collective-permute-start.2 = (bf16[128,1664]{1,0:T(8,128)(2,1)S(1)}, bf16[128,1664]{1,0:T(8,128)(2,1)}, u32[]{:S(2)}, u32[]{:S(2)}) collective-permute-start(bf16[128,1664]{1,0:T(8,128)(2,1)S(1)} %collective-permute-done.refs_1_), channel_id=1, source_target_pairs={{0,1},{1,0},{2,3},{3,2},{4,5},{5,4},{6,7},{7,6},{8,9},{9,8},{10,11... | collective-permute-start | bytes 1277960 | tf_op jit(solution)/shard_map/ppermute | solution.py:335
  81.3 2.9 %collective-permute-start.9 = (bf16[128,1664]{1,0:T(8,128)(2,1)}, bf16[128,1664]{1,0:T(8,128)(2,1)}, u32[]{:S(2)}, u32[]{:S(2)}) collective-permute-start(bf16[128,1664]{1,0:T(8,128)(2,1)} %collective-permute-done.7.refs_0_), channel_id=1, source_target_pairs={{0,1},{1,0},{2,3},{3,2},{4,5},{5,4},{6,7},{7,6},{8,9},{9,8},{10,11... | collective-permute-start | bytes 1277960 | tf_op jit(solution)/shard_map/ppermute | solution.py:335
  82.5 2.7 collective-permute-start.10
  84.2 19.1 %collective-permute-start.22 = (bf16[128,3072]{1,0:T(8,128)(2,1)}, bf16[128,3072]{1,0:T(8,128)(2,1)}, u32[]{:S(2)}, u32[]{:S(2)}) collective-permute-start(bf16[128,3072]{1,0:T(8,128)(2,1)} %add_convert_fusion.3), channel_id=1, source_target_pairs={{0,2},{1,3},{2,0},{3,1},{4,6},{5,7},{6,4},{7,5},{8,10},{9,11},{10,... | collective-permute-start | bytes 2359304 | tf_op jit(solution)/shard_map/ppermute | solution.py:335
  96.3 23.1 %collective-permute-start.11 = (bf16[256,3072]{1,0:T(8,128)(2,1)}, bf16[256,3072]{1,0:T(8,128)(2,1)}, u32[]{:S(2)}, u32[]{:S(2)}) collective-permute-start(bf16[256,3072]{1,0:T(8,128)(2,1)} %get-tuple-element.32), channel_id=1, source_target_pairs={{0,1},{1,0},{2,3},{3,2},{4,5},{5,4},{6,7},{7,6},{8,9},{9,8},{10,11... | collective-permute-start | bytes 4718600 | tf_op jit(solution)/shard_map/ppermute | solution.py:335
  97.2 24.6 %collective-permute-start.17 = (bf16[128,3072]{1,0:T(8,128)(2,1)S(1)}, bf16[128,3072]{1,0:T(8,128)(2,1)}, u32[]{:S(2)}, u32[]{:S(2)}) collective-permute-start(bf16[128,3072]{1,0:T(8,128)(2,1)S(1)} %add_convert_fusion.4), channel_id=1, source_target_pairs={{0,2},{1,3},{2,0},{3,1},{4,6},{5,7},{6,4},{7,5},{8,10},{9,11},{10,... | collective-permute-start | bytes 2359304 | tf_op jit(solution)/shard_map/ppermute | solution.py:335
  105.7 19.5 %collective-permute-start.23 = (bf16[128,3072]{1,0:T(8,128)(2,1)}, bf16[128,3072]{1,0:T(8,128)(2,1)S(1)}, u32[]{:S(2)}, u32[]{:S(2)}) collective-permute-start(bf16[128,3072]{1,0:T(8,128)(2,1)} %add_convert_fusion.2), channel_id=1, source_target_pairs={{0,4},{1,5},{2,6},{3,7},{4,8},{5,9},{6,10},{7,11},{8,12},{9,13},{1... | collective-permute-start | bytes 2359304 | tf_op jit(solution)/shard_map/ppermute | solution.py:335
  117.3 9.6 %collective-permute-start.3 = (bf16[256,3072]{1,0:T(8,128)(2,1)}, bf16[256,3072]{1,0:T(8,128)(2,1)S(1)}, u32[]{:S(2)}, u32[]{:S(2)}) collective-permute-start(bf16[256,3072]{1,0:T(8,128)(2,1)} %get-tuple-element.30), channel_id=1, source_target_pairs={{0,1},{1,0},{2,3},{3,2},{4,5},{5,4},{6,7},{7,6},{8,9},{9,8},{10,11... | collective-permute-start | bytes 4718600 | tf_op jit(solution)/shard_map/ppermute | solution.py:335
  120.7 19.2 %collective-permute-start.12 = (bf16[128,3072]{1,0:T(8,128)(2,1)S(1)}, bf16[128,3072]{1,0:T(8,128)(2,1)S(1)}, u32[]{:S(2)}, u32[]{:S(2)}) collective-permute-start(bf16[128,3072]{1,0:T(8,128)(2,1)S(1)} %add_convert_fusion.5), channel_id=1, source_target_pairs={{0,2},{1,3},{2,0},{3,1},{4,6},{5,7},{6,4},{7,5},{8,10},{9,11},{10,... | collective-permute-start | bytes 2359304 | tf_op jit(solution)/shard_map/ppermute | solution.py:335
  126.9 18.0 %collective-permute-start.24 = (bf16[128,3072]{1,0:T(8,128)(2,1)S(1)}, bf16[128,3072]{1,0:T(8,128)(2,1)S(1)}, u32[]{:S(2)}, u32[]{:S(2)}) collective-permute-start(bf16[128,3072]{1,0:T(8,128)(2,1)S(1)} %add_convert_fusion.1), channel_id=1, source_target_pairs={{0,4},{1,5},{2,6},{3,7},{4,8},{5,9},{6,10},{7,11},{8,12},{9,13},{1... | collective-permute-start | bytes 2359304 | tf_op jit(solution)/shard_map/ppermute | solution.py:335
  127.1 29.7 %collective-permute-start.4 = (bf16[128,3072]{1,0:T(8,128)(2,1)S(1)}, bf16[128,3072]{1,0:T(8,128)(2,1)S(1)}, u32[]{:S(2)}, u32[]{:S(2)}) collective-permute-start(bf16[128,3072]{1,0:T(8,128)(2,1)S(1)} %add_convert_fusion.6), channel_id=1, source_target_pairs={{0,2},{1,3},{2,0},{3,1},{4,6},{5,7},{6,4},{7,5},{8,10},{9,11},{10,... | collective-permute-start | bytes 2359304 | tf_op jit(solution)/shard_map/ppermute | solution.py:335
  146.5 17.0 %collective-permute-start.25 = (bf16[128,3072]{1,0:T(8,128)(2,1)S(1)}, bf16[128,3072]{1,0:T(8,128)(2,1)S(1)}, u32[]{:S(2)}, u32[]{:S(2)}) collective-permute-start(bf16[128,3072]{1,0:T(8,128)(2,1)S(1)} %add_convert_fusion), channel_id=1, source_target_pairs={{0,4},{1,5},{2,6},{3,7},{4,8},{5,9},{6,10},{7,11},{8,12},{9,13},{1... | collective-permute-start | bytes 2359304 | tf_op jit(solution)/shard_map/ppermute | solution.py:335
  164.2 87.4 %copy-start.9 = (bf16[128,3072]{1,0:T(8,128)(2,1)}, bf16[128,3072]{1,0:T(8,128)(2,1)S(1)}, u32[]{:S(2)}) copy-start(bf16[128,3072]{1,0:T(8,128)(2,1)S(1)} %pad_maximum_fusion.refs_0_) | copy-start | bytes 2359300
  164.2 16.1 %collective-permute-start.26 = (bf16[128,3072]{1,0:T(8,128)(2,1)S(1)}, bf16[128,3072]{1,0:T(8,128)(2,1)S(1)}, u32[]{:S(2)}, u32[]{:S(2)}) collective-permute-start(bf16[128,3072]{1,0:T(8,128)(2,1)S(1)} %pad_maximum_fusion.refs_0_), channel_id=1, source_target_pairs={{0,4},{1,5},{2,6},{3,7},{4,8},{5,9},{6,10},{7,11},{8,12},{9,13},{1... | collective-permute-start | bytes 2359304 | tf_op jit(solution)/shard_map/ppermute | solution.py:335
  164.3 22.5 %collective-permute-start.32 = (bf16[128,3072]{1,0:T(8,128)(2,1)S(1)}, bf16[128,3072]{1,0:T(8,128)(2,1)S(1)}, u32[]{:S(2)}, u32[]{:S(2)}) collective-permute-start(bf16[128,3072]{1,0:T(8,128)(2,1)S(1)} %pad_maximum_fusion.refs_0_), channel_id=1, source_target_pairs={{0,2},{1,3},{2,0},{3,1},{4,6},{5,7},{6,4},{7,5},{8,10},{9,11},{10,... | collective-permute-start | bytes 2359304 | tf_op jit(solution)/shard_map/ppermute | solution.py:335
  180.3 71.3 %copy-start.21 = (bf16[128,3072]{1,0:T(8,128)(2,1)}, bf16[128,3072]{1,0:T(8,128)(2,1)S(1)}, u32[]{:S(2)}) copy-start(bf16[128,3072]{1,0:T(8,128)(2,1)S(1)} %collective-permute-done.26.refs_4_) | copy-start | bytes 2359300
  180.3 16.0 %collective-permute-start.27 = (bf16[128,3072]{1,0:T(8,128)(2,1)S(1)}, bf16[128,3072]{1,0:T(8,128)(2,1)S(1)}, u32[]{:S(2)}, u32[]{:S(2)}) collective-permute-start(bf16[128,3072]{1,0:T(8,128)(2,1)S(1)} %collective-permute-done.26.refs_4_), channel_id=1, source_target_pairs={{0,4},{1,5},{2,6},{3,7},{4,8},{5,9},{6,10},{7,11},{8,12},{9,13},{1... | collective-permute-start | bytes 2359304 | tf_op jit(solution)/shard_map/ppermute | solution.py:335
  180.3 17.7 %collective-permute-start.33 = (bf16[128,3072]{1,0:T(8,128)(2,1)S(1)}, bf16[128,3072]{1,0:T(8,128)(2,1)S(1)}, u32[]{:S(2)}, u32[]{:S(2)}) collective-permute-start(bf16[128,3072]{1,0:T(8,128)(2,1)S(1)} %pad_maximum_fusion.refs_0_), channel_id=1, source_target_pairs={{0,1},{1,0},{2,3},{3,2},{4,5},{5,4},{6,7},{7,6},{8,9},{9,8},{10,11... | collective-permute-start | bytes 2359304 | tf_op jit(solution)/shard_map/ppermute | solution.py:335
  186.7 64.9 %copy-start.22 = (bf16[128,3072]{1,0:T(8,128)(2,1)}, bf16[128,3072]{1,0:T(8,128)(2,1)S(1)}, u32[]{:S(2)}) copy-start(bf16[128,3072]{1,0:T(8,128)(2,1)S(1)} %collective-permute-done.32.refs_1_) | copy-start | bytes 2359300
  186.7 19.8 %collective-permute-start.34 = (bf16[128,3072]{1,0:T(8,128)(2,1)S(1)}, bf16[128,3072]{1,0:T(8,128)(2,1)S(1)}, u32[]{:S(2)}, u32[]{:S(2)}) collective-permute-start(bf16[128,3072]{1,0:T(8,128)(2,1)S(1)} %collective-permute-done.32.refs_1_), channel_id=1, source_target_pairs={{0,1},{1,0},{2,3},{3,2},{4,5},{5,4},{6,7},{7,6},{8,9},{9,8},{10,11... | collective-permute-start | bytes 2359304 | tf_op jit(solution)/shard_map/ppermute | solution.py:335
  196.3 55.3 %copy-start.23 = (bf16[128,3072]{1,0:T(8,128)(2,1)}, bf16[128,3072]{1,0:T(8,128)(2,1)S(1)}, u32[]{:S(2)}) copy-start(bf16[128,3072]{1,0:T(8,128)(2,1)S(1)} %collective-permute-done.27.refs_8_) | copy-start | bytes 2359300
  196.3 16.0 %collective-permute-start.28 = (bf16[128,3072]{1,0:T(8,128)(2,1)S(1)}, bf16[128,3072]{1,0:T(8,128)(2,1)S(1)}, u32[]{:S(2)}, u32[]{:S(2)}) collective-permute-start(bf16[128,3072]{1,0:T(8,128)(2,1)S(1)} %collective-permute-done.27.refs_8_), channel_id=1, source_target_pairs={{0,4},{1,5},{2,6},{3,7},{4,8},{5,9},{6,10},{7,11},{8,12},{9,13},{1... | collective-permute-start | bytes 2359304 | tf_op jit(solution)/shard_map/ppermute | solution.py:335
  196.5 16.8 %collective-permute-start.35 = (bf16[128,3072]{1,0:T(8,128)(2,1)S(1)}, bf16[128,3072]{1,0:T(8,128)(2,1)S(1)}, u32[]{:S(2)}, u32[]{:S(2)}) collective-permute-start(bf16[128,3072]{1,0:T(8,128)(2,1)S(1)} %collective-permute-done.26.refs_4_), channel_id=1, source_target_pairs={{0,2},{1,3},{2,0},{3,1},{4,6},{5,7},{6,4},{7,5},{8,10},{9,11},{10,... | collective-permute-start | bytes 2359304 | tf_op jit(solution)/shard_map/ppermute | solution.py:335
  197.5 27.5 %collective-permute-start.38 = (bf16[128,3072]{1,0:T(8,128)(2,1)S(1)}, bf16[128,3072]{1,0:T(8,128)(2,1)S(1)}, u32[]{:S(2)}, u32[]{:S(2)}) collective-permute-start(bf16[128,3072]{1,0:T(8,128)(2,1)S(1)} %collective-permute-done.27.refs_8_), channel_id=1, source_target_pairs={{0,2},{1,3},{2,0},{3,1},{4,6},{5,7},{6,4},{7,5},{8,10},{9,11},{10,... | collective-permute-start | bytes 2359304 | tf_op jit(solution)/shard_map/ppermute | solution.py:335
  198.0 53.6 %copy-start.24 = (bf16[128,3072]{1,0:T(8,128)(2,1)}, bf16[128,3072]{1,0:T(8,128)(2,1)S(1)}, u32[]{:S(2)}) copy-start(bf16[128,3072]{1,0:T(8,128)(2,1)S(1)} %collective-permute-done.33.refs_2_) | copy-start | bytes 2359300
  198.0 43.8 %collective-permute-start.36 = (bf16[128,3072]{1,0:T(8,128)(2,1)S(1)}, bf16[128,3072]{1,0:T(8,128)(2,1)}, u32[]{:S(2)}, u32[]{:S(2)}) collective-permute-start(bf16[128,3072]{1,0:T(8,128)(2,1)S(1)} %collective-permute-done.26.refs_4_), channel_id=1, source_target_pairs={{0,1},{1,0},{2,3},{3,2},{4,5},{5,4},{6,7},{7,6},{8,9},{9,8},{10,11... | collective-permute-start | bytes 2359304 | tf_op jit(solution)/shard_map/ppermute | solution.py:335
  206.6 43.7 %collective-permute-start.39 = (bf16[128,3072]{1,0:T(8,128)(2,1)S(1)}, bf16[128,3072]{1,0:T(8,128)(2,1)S(1)}, u32[]{:S(2)}, u32[]{:S(2)}) collective-permute-start(bf16[128,3072]{1,0:T(8,128)(2,1)S(1)} %collective-permute-done.27.refs_8_), channel_id=1, source_target_pairs={{0,1},{1,0},{2,3},{3,2},{4,5},{5,4},{6,7},{7,6},{8,9},{9,8},{10,11... | collective-permute-start | bytes 2359304 | tf_op jit(solution)/shard_map/ppermute | solution.py:335
  212.3 62.7 %copy-start.5 = (bf16[128,3072]{1,0:T(8,128)(2,1)}, bf16[128,3072]{1,0:T(8,128)(2,1)S(1)}, u32[]{:S(2)}) copy-start(bf16[128,3072]{1,0:T(8,128)(2,1)S(1)} %collective-permute-done.28.refs_0_) | copy-start | bytes 2359300
  212.3 29.5 %collective-permute-start.29 = (bf16[128,3072]{1,0:T(8,128)(2,1)S(1)}, bf16[128,3072]{1,0:T(8,128)(2,1)S(1)}, u32[]{:S(2)}, u32[]{:S(2)}) collective-permute-start(bf16[128,3072]{1,0:T(8,128)(2,1)S(1)} %collective-permute-done.28.refs_0_), channel_id=1, source_target_pairs={{0,2},{1,3},{2,0},{3,1},{4,6},{5,7},{6,4},{7,5},{8,10},{9,11},{10,... | collective-permute-start | bytes 2359304 | tf_op jit(solution)/shard_map/ppermute | solution.py:335
  213.3 36.9 %collective-permute-start.37 = (bf16[128,3072]{1,0:T(8,128)(2,1)S(1)}, bf16[128,3072]{1,0:T(8,128)(2,1)S(1)}, u32[]{:S(2)}, u32[]{:S(2)}) collective-permute-start(bf16[128,3072]{1,0:T(8,128)(2,1)S(1)} %collective-permute-done.35.refs_5_), channel_id=1, source_target_pairs={{0,1},{1,0},{2,3},{3,2},{4,5},{5,4},{6,7},{7,6},{8,9},{9,8},{10,11... | collective-permute-start | bytes 2359304 | tf_op jit(solution)/shard_map/ppermute | solution.py:335
  225.0 25.2 %collective-permute-start.40 = (bf16[128,3072]{1,0:T(8,128)(2,1)S(1)}, bf16[128,3072]{1,0:T(8,128)(2,1)S(1)}, u32[]{:S(2)}, u32[]{:S(2)}) collective-permute-start(bf16[128,3072]{1,0:T(8,128)(2,1)S(1)} %collective-permute-done.38.refs_9_), channel_id=1, source_target_pairs={{0,1},{1,0},{2,3},{3,2},{4,5},{5,4},{6,7},{7,6},{8,9},{9,8},{10,11... | collective-permute-start | bytes 2359304 | tf_op jit(solution)/shard_map/ppermute | solution.py:335
  241.8 33.3 %collective-permute-start.30 = (bf16[128,3072]{1,0:T(8,128)(2,1)S(1)}, bf16[128,3072]{1,0:T(8,128)(2,1)S(1)}, u32[]{:S(2)}, u32[]{:S(2)}) collective-permute-start(bf16[128,3072]{1,0:T(8,128)(2,1)S(1)} %collective-permute-done.28.refs_0_), channel_id=1, source_target_pairs={{0,1},{1,0},{2,3},{3,2},{4,5},{5,4},{6,7},{7,6},{8,9},{9,8},{10,11... | collective-permute-start | bytes 2359304 | tf_op jit(solution)/shard_map/ppermute | solution.py:335
  241.9 33.2 %collective-permute-start.31 = (bf16[128,3072]{1,0:T(8,128)(2,1)S(1)}, bf16[128,3072]{1,0:T(8,128)(2,1)S(1)}, u32[]{:S(2)}, u32[]{:S(2)}) collective-permute-start(bf16[128,3072]{1,0:T(8,128)(2,1)S(1)} %collective-permute-done.29.refs_1_), channel_id=1, source_target_pairs={{0,1},{1,0},{2,3},{3,2},{4,5},{5,4},{6,7},{7,6},{8,9},{9,8},{10,11... | collective-permute-start | bytes 2359304 | tf_op jit(solution)/shard_map/ppermute | solution.py:335
  (24 other events, 305.4 us)
